TPU v7x, 256 devices: a whole 4x4x8 slice. The times are simulated.
256 devices in a mesh: trc: 4 (over y), lat: 4 (over x_lo, core), lon: 16 (over x_hi, z).
Axes of the slice: x: 4 (x_hi: 2, x_lo: 2; x = x_hi * 2 + x_lo), y: 4, z: 8, core: 2. Of those that a mesh axis runs over, the one named last changes fastest.
Arguments:
- species_concentrations: float32 [32, 8, 128, 2048], P('trc', None, 'lat', 'lon'), may hold values from 0.2 to 4
- zonal_velocity_array: float32 [8, 128, 2048], P('trc', 'lat', 'lon'), may hold values from -2.5 to 2.5
- meridional_velocity_array: float32 [8, 128, 2048], P('trc', 'lat', 'lon'), may hold values from -2.5 to 2.5
- thermal_anomaly: float32 [8, 128, 2048], P('trc', 'lat', 'lon'), may hold values from -6 to 6
- ocean_top_height_grid: float32 [128, 2048], P('lat', 'lon'), may hold values from -6 to 6
- water_layer_tally: int32 [128, 2048], P('lat', 'lon'), may hold values from 0 to 8
- species_interaction_table: float32 [32, 32], replicated, may hold values from -1 to 1
- species_production_pace: float32 [32], replicated, may hold values from 0.2 to 2
- photon_uptake: float32 [32], replicated, may hold values from 0.01 to 0.1
Outputs:
- updated_tracers: float32 [32, 8, 128, 2048], P('trc', None, 'lat', 'lon')
- east_out: float32 [8, 128, 2048], P('trc', 'lat', 'lon')
- north_out: float32 [8, 128, 2048], P('trc', 'lat', 'lon')
- temperature_out: float32 [8, 128, 2048], P('trc', 'lat', 'lon')
- height_out: float32 [128, 2048], P('lat', 'lon')
Inputs may be any that keep to these rules, and one draw needn't show every extreme that they name: `water_layer_tally`: the number of wet levels of a column, counted from the surface; cells below it, and whole columns with 0, are land.
All inputs are finite; a program needn't handle non-finite values.
Results may differ from a plain program's by a relative error of at most 0.0003.
Values sent between devices are 32-bit elements; how exact they have to be, the bound alone decides.
A program may use at most 64 MiB of HBM per device.

v0:
```python
import functools
import math

import jax
import jax.numpy as jnp
from jax import lax
from jax.experimental import pallas as pl
from jax.experimental.pallas import tpu as pltpu
from jax.sharding import PartitionSpec as P

MESH = pl.DeviceIdType.MESH
F32 = jnp.float32
DT = 0.1
CHUNKS = ((0, 12), (12, 20))
HALO = 4
UNROLL = 4


def in_pieces(rows):
    pieces = [(0, HALO), (rows - HALO, HALO)]
    need, done = [], HALO
    for first, count in CHUNKS:
        end = min(first + count + HALO, rows - HALO)
        if end > done:
            pieces.append((done, end - done))
            done = end
        need.append(len(pieces))
    return pieces, need


def minmod(x, y):
    return jnp.maximum(jnp.minimum(x, y), jnp.minimum(jnp.maximum(x, y), 0.0))


def lanes(x, shift):
    shift = shift % x.shape[-1]
    return pltpu.roll(x, shift, x.ndim - 1) if shift else x


def rows_by(x, shift):
    shift = -shift % x.shape[0]
    return pltpu.roll(x, shift, 0) if shift else x


def kernel(
    x, u_in, v_in, th_in, h_in, w_in, table, pace, uptake,
    o_x, o_u, o_v, o_t, o_h,
    tx, c0, c1, c2, out, ry, pk_own, pk_got, cc, cf,
    vs, mom, dp, dp_got, h1, ab, s_own, s_got, fl, w01, prod,
    in_s, in_r, lon_s, lon_r, lat_s, lat_r, vs_s, vs_r, dp_s, dp_r, h_s, h_r,
    s_s, s_r, out_s, out_r, loc,
):
    rows, width = h_in.shape
    n_lat, n_lon = lax.axis_size("lat"), lax.axis_size("lon")
    t, la, lo = lax.axis_index("trc"), lax.axis_index("lat"), lax.axis_index("lon")
    other = [lax.rem(t + d, 4) for d in (1, 2, 3)]
    source = [lax.rem(t + 4 - d, 4) for d in (1, 2, 3)]
    east, west = lax.rem(lo + 1, n_lon), lax.rem(lo + n_lon - 1, n_lon)
    north, south = lax.rem(la + 1, n_lat), lax.rem(la + n_lat - 1, n_lat)
    pieces, need = in_pieces(rows)

    def remote(src, dst, send, recv, where):
        return pltpu.make_async_remote_copy(
            src_ref=src, dst_ref=dst, send_sem=send, recv_sem=recv, device_id=where, device_id_type=MESH
        )

    sends = []

    def go(copy):
        copy.start()
        sends.append(copy)
        return copy

    barrier = pltpu.get_barrier_semaphore()
    friends = [{"trc": g} for g in other] + [{"lon": east}, {"lon": west}, {"lat": north}, {"lat": south}]
    for friend in friends:
        pl.semaphore_signal(barrier, inc=1, device_id=friend, device_id_type=MESH)

    depth = w_in[...].astype(F32)

    def wet_of(level, depths):
        return jnp.where(level < depths, 1.0, 0.0)

    own = pl.ds(8, rows)
    for kk in range(2):
        wet = wet_of((2 * t + kk).astype(F32), depth)
        vs[1, kk, own] = wet * u_in[kk]
        vs[1, 2 + kk, own] = wet * v_in[kk]
    vs[1, 4, own] = h_in[...]
    vs[1, 5, own] = depth

    def turn(target, dst, base):
        for kk in range(2):
            for n in range(8):
                dst[kk, pl.ds(base + n, rows, stride=8), :] = x[n, 2 * target + kk]

    pl.semaphore_wait(barrier, len(friends))
    vs_lon = [
        go(remote(vs.at[1, :, own], vs.at[0, :, own], vs_s.at[0], vs_r.at[0], {"lon": east})),
        go(remote(vs.at[1, :, own], vs.at[2, :, own], vs_s.at[1], vs_r.at[1], {"lon": west})),
    ]
    incoming = {}

    def send_piece(d, p):
        first, count = pieces[p]
        incoming[d, p] = go(
            remote(
                tx.at[d, :, pl.ds(8 * first, 8 * count)],
                c0.at[t, :, pl.ds(8 * (first + HALO), 8 * count)],
                in_s.at[d, p], in_r.at[d, p], {"trc": other[d]},
            )
        )

    for d in (1, 0, 2):
        turn(other[d], tx.at[d], 0)
        send_piece(d, 0)
        send_piece(d, 1)
    turn(t, c0.at[t], 8 * HALO)
    for p in range(2, len(pieces)):
        for d in (1, 0, 2):
            send_piece(d, p)

    for copy in vs_lon:
        copy.wait_recv()
    top, low = pl.ds(rows, 8), pl.ds(8, 8)
    vs_lat = [
        go(remote(vs.at[:, :, top], vs.at[:, :, pl.ds(0, 8)], vs_s.at[2], vs_r.at[2], {"lat": north})),
        go(remote(vs.at[:, :, low], vs.at[:, :, pl.ds(rows + 8, 8)], vs_s.at[3], vs_r.at[3], {"lat": south})),
    ]

    lane = lax.broadcasted_iota(jnp.int32, (8, width), 1)
    slot = lane // 8
    lane32 = lane % 32

    def tile(buf, g, kk, r):
        return buf[g, kk, pl.ds(pl.multiple_of(8 * (r + HALO), 8), 8), :]

    def pack(q):
        pos = (q + 1) % (rows // 4)
        for kk in range(2):
            to_west = to_east = jnp.zeros((8, width), F32)
            for j in range(4):
                for g in range(4):
                    s = 4 * g + j
                    turned = lanes(tile(c0, g, kk, 4 * q + j), 8 * (s + 1))
                    to_west = jnp.where(slot == (s + 1) % 16, turned, to_west)
                    to_east = jnp.where(slot == s, turned, to_east)
            pk_own[0, kk, pos] = to_west
            pk_own[1, kk, pos] = to_east

    def send_pack(i, quads):
        pos = [(q + 1) % (rows // 4) for q in quads]
        part = pl.ds(min(pos), len(pos))
        return [
            go(remote(pk_own.at[1, :, part], pk_got.at[1, :, part], lon_s.at[0, i], lon_r.at[0, i], {"lon": east})),
            go(remote(pk_own.at[0, :, part], pk_got.at[0, :, part], lon_s.at[1, i], lon_r.at[1, i], {"lon": west})),
        ]

    def strips(q):
        pos = (q + 1) % (rows // 4)
        for kk in range(2):
            from_west, from_east = pk_got[1, kk, pos], pk_got[0, kk, pos]
            own_w, own_e = pk_own[0, kk, pos], pk_own[1, kk, pos]
            for j in range(4):
                left = lanes(jnp.where(slot % 4 == j, from_west, own_w), -8 * j)
                right = lanes(jnp.where(slot % 4 == j, own_e, from_east), 16 - 8 * j)
                c0[4, kk, pl.ds(8 * (4 * q + j + HALO), 8), :] = jnp.where(lane32 < 16, left, right)

    for p in (0, 1):
        for d in range(3):
            incoming[d, p].wait_recv()
    last = rows // 4 - 1
    pack(last)
    pack(0)
    pk = send_pack(0, (last, 0))

    for copy in vs_lat:
        copy.wait_recv()

    @pl.when(la == 0)
    def _():
        for b in range(3):
            for f in range(6):
                vs[b, f, 0:8] = jnp.zeros((8, width), F32)

    @pl.when(la == n_lat - 1)
    def _():
        for b in range(3):
            for f in range(6):
                vs[b, f, rows + 8 : rows + 16] = jnp.zeros((8, width), F32)

    vlane = lax.broadcasted_iota(jnp.int32, (rows + 16, width), 1) % 32

    def strip_form(f):
        w_, o_, e_ = vs[0, f], vs[1, f], vs[2, f]
        left = jnp.where(vlane < 8, lanes(w_, 8), lanes(o_, 8))
        right = jnp.where(vlane < 24, lanes(o_, 24), lanes(e_, 24))
        first = jnp.where(vlane < 16, left, right)
        lane_ = lax.broadcasted_iota(jnp.int32, first.shape, 1)
        first = jnp.where(lane_ < 32, first, 0.0)
        first = first + lanes(first, 32)
        return first + lanes(first, 64)

    def weights(a):
        ap, an = jnp.maximum(a, 0.0), jnp.minimum(a, 0.0)
        return ap, 0.5 * ap * (1.0 - ap), an, -0.5 * an * (1.0 + an)

    for form in range(2):
        get = (lambda f: vs[1, f]) if form == 0 else strip_form
        dep = get(5)
        for kk in range(2):
            wet = wet_of((2 * t + kk).astype(F32), dep)
            u, v = get(kk), get(2 + kk)
            ax = 0.5 * (u + lanes(u, -1)) * wet * lanes(wet, -1)
            ap, bp, an, bn = weights(ax)
            cc[form, 0, kk], cc[form, 1, kk] = ap, bp
            cc[form, 2, kk], cc[form, 3, kk] = lanes(an, 1), lanes(bn, 1)
            ay = 0.5 * (v + rows_by(v, 1)) * wet * rows_by(wet, 1)
            for i, w in enumerate(weights(ay)):
                cc[form, 4 + i, kk] = w

    @pl.loop(1, rows + 2 * HALO)
    def _(r):
        for form in range(2):
            for i in range(8):
                for kk in range(2):
                    cf[form, i, kk, r] = jnp.broadcast_to(cc[form, i, kk, pl.ds(r + 8 - HALO, 1), :], (8, width))

    big = rows + 16
    row_no = (la * rows - 8 + lax.broadcasted_iota(jnp.int32, (big, 1), 0)).astype(F32)
    angle = math.pi * ((row_no + 0.5) / (rows * n_lat) - 0.5)
    coriolis = 0.5 * jnp.sin(angle)
    surface = 1.0 + jnp.cos(angle)
    wide = lambda ref, f: jnp.concatenate([ref[0, f], ref[1, f], ref[2, f]], axis=1)

    def momentum(u, v, h, wet):
        h_x = 0.5 * (lanes(h, -1) - lanes(h, 1))
        h_y = 0.5 * (rows_by(h, 1) - rows_by(h, -1))
        lap_u = rows_by(u, 1) + rows_by(u, -1) + lanes(u, -1) + lanes(u, 1) - 4.0 * u
        lap_v = rows_by(v, 1) + rows_by(v, -1) + lanes(v, -1) + lanes(v, 1) - 4.0 * v
        new_u = wet * (u + DT * (coriolis * v - h_x + 0.2 * lap_u - 0.05 * u))
        new_v = wet * (v + DT * (-coriolis * u - h_y + 0.2 * lap_v - 0.05 * v))
        return new_u, new_v

    def divergence(u, v):
        d = 0.5 * (lanes(u, -1) - lanes(u, 1)) + 0.5 * (rows_by(v, 1) - rows_by(v, -1))
        return d[8 : 8 + rows, width : 2 * width]

    def dp_stage(i):
        partner = t + 1 - 2 * lax.rem(t, 2) if i % 2 == 0 else 3 - t
        return go(remote(dp.at[i], dp_got.at[i], dp_s.at[i], dp_r.at[i], {"trc": partner}))

    wide_depth = wide(vs, 5)
    wide_h = wide(vs, 4)
    div = jnp.zeros((rows, width), F32)
    for kk in range(2):
        u, v = wide(vs, kk), wide(vs, 2 + kk)
        div = div + divergence(u, v)
        mom[kk], mom[2 + kk] = momentum(u, v, wide_h, wet_of((2 * t + kk).astype(F32), wide_depth))
    dp[0] = div
    stage = dp_stage(0)

    for copy in pk:
        copy.wait_recv()
    strips(last)
    strips(0)
    lat = [
        go(remote(c0.at[:, :, pl.ds(8 * rows, 8 * HALO)], c0.at[:, :, pl.ds(0, 8 * HALO)],
                  lat_s.at[0], lat_r.at[0], {"lat": north})),
        go(remote(c0.at[:, :, pl.ds(8 * HALO, 8 * HALO)], c0.at[:, :, pl.ds(8 * (rows + HALO), 8 * HALO)],
                  lat_s.at[1], lat_r.at[1], {"lat": south})),
    ]
    stage.wait_recv()
    dp[1] = dp[0] + dp_got[0]
    stage = dp_stage(1)

    sub = lax.broadcasted_iota(jnp.int32, (8, width), 0)

    def column(ref, g):
        col = jnp.full((8, width), ref[8 * g], F32)
        for n in range(1, 8):
            col = jnp.where(sub == n, ref[8 * g + n], col)
        return col

    uptakes = [column(uptake, g) for g in range(4)]
    for g in range(4):
        prod[g] = column(pace, g)

    def step(src, dst, first, count, finish):
        for kk in range(2):
            def coef(form, i, r):
                return cf[form, i, kk, r + HALO]

            def face_y(form, r, a, s_a, b, s_b):
                return (coef(form, 4, r) * a + coef(form, 5, r) * s_a) + (coef(form, 6, r) * b + coef(form, 7, r) * s_b)

            start = []
            for g in range(5):
                q = [tile(src, g, kk, first + i) for i in (-2, -1, 0, 1)]
                d = [q[i + 1] - q[i] for i in range(3)]
                s = [minmod(d[0], d[1]), minmod(d[1], d[2])]
                start.append((q[2], q[3], d[2], s[1], face_y(g // 4, first - 1, q[1], s[0], q[2], s[1])))

            def one(r, state):
                result, after = [], []
                for g in range(5):
                    form = g // 4
                    c, c_n, d_n, s, g_s = state[g]
                    c_nn = tile(src, g, kk, r + 2)
                    d_nn = c_nn - c_n
                    s_n = minmod(d_nn, d_n)
                    g_n = face_y(form, r, c, s, c_n, s_n)
                    d_e = lanes(c, -1) - c
                    s_x = minmod(d_e, lanes(d_e, 1))
                    right = coef(form, 0, r) * c + coef(form, 1, r) * s_x
                    left = coef(form, 2, r) * c + coef(form, 3, r) * s_x
                    new = c - ((right + lanes(left, -1)) - (lanes(right, 1) + left)) - (g_n - g_s)
                    result.append(new)
                    after.append((c_n, c_nn, d_nn, s_n, g_n))
                if finish:
                    total = jnp.zeros((8, width), F32)
                    for g in range(4):
                        new = jnp.where(lane < 4, lanes(result[4], -(32 * g + 8)), result[g])
                        new = jnp.where(lane >= width - 4, lanes(result[4], width - 24 - 32 * g), new)
                        dst[g, kk, pl.ds(pl.multiple_of(8 * (r + HALO), 8), 8), :] = new
                        total = total + uptakes[g] * jnp.abs(new)
                    ab[kk, pl.ds(r, 1), :] = jnp.sum(total, axis=0, keepdims=True)
                else:
                    for g in range(5):
                        dst[g, kk, pl.ds(pl.multiple_of(8 * (r + HALO), 8), 8), :] = result[g]
                return tuple(after)

            def some(i, state):
                for j in range(UNROLL):
                    state = one(first + UNROLL * i + j, state)
                return state

            lax.fori_loop(0, count // UNROLL, some, tuple(start))

    def layer(kk, first, count):
        dep = vs[1, 5, pl.ds(8 + first, count)]
        wet = wet_of((2 * t + kk).astype(F32), dep)
        return 0.25 * (0.2 + ab[kk, pl.ds(first, count)]) * wet, wet

    def send_layers(c):
        first, count = CHUNKS[c]
        s_own[c, 0:count] = layer(0, first, count)[0] + layer(1, first, count)[0]
        return [
            go(remote(s_own.at[c], s_got.at[c, d], s_s.at[c, d], s_r.at[c, d], {"trc": other[d]}))
            for d in range(3)
        ]

    def finish_chunk(c):
        first, count = CHUNKS[c]
        above = jnp.zeros((count, width), F32)
        for d in range(3):
            above = above + jnp.where(t - (d + 1) >= 0, 1.0, 0.0) * s_got[c, d, 0:count]
        light_in = surface[8 + first : 8 + first + count]
        part = pl.ds(first, count)
        for kk in range(2):
            lay, wet = layer(kk, first, count)
            over = light_in * jnp.exp(-above)
            o_t[kk, part] = th_in[kk, part] + over * (1.0 - jnp.exp(-lay))
            fl[kk, part] = DT * wet * (over / (over + 0.5))
            w01[kk, part] = DT * wet
            above = above + lay
        matrix = table[...]

        @pl.loop(0, count // 4)
        def _(i):
            for kk in range(2):
                r0 = first + 4 * i
                stacked = jnp.concatenate(
                    [jnp.concatenate([tile(c2, g, kk, r0 + j) for g in range(4)], axis=0) for j in range(4)], axis=1
                )
                mixed = jnp.dot(matrix, stacked, precision=lax.Precision.HIGHEST, preferred_element_type=F32)
                for j in range(4):
                    light = fl[kk, pl.ds(r0 + j, 1), :]
                    wet = w01[kk, pl.ds(r0 + j, 1), :]
                    for g in range(4):
                        moved = tile(c2, g, kk, r0 + j)
                        mix = mixed[8 * g : 8 * g + 8, width * j : width * (j + 1)]
                        out[g, kk, pl.ds(pl.multiple_of(8 * (r0 + j), 8), 8), :] = (
                            moved + wet * mix + light * (prod[g] * moved)
                        )

        part8 = pl.ds(8 * first, 8 * count)
        copies = [
            go(remote(out.at[other[d], :, part8], ry.at[t, :, part8], out_s.at[c, d], out_r.at[c, d], {"trc": other[d]}))
            for d in (1, 0, 2)
        ]
        here = pltpu.make_async_copy(out.at[t, :, part8], ry.at[t, :, part8], loc.at[c])
        here.start()
        return copies, here

    zero_tile = jnp.zeros((8, width), F32)
    done_pieces, done_quads = 2, 1
    layers = [None] * len(CHUNKS)
    results = [None] * len(CHUNKS)
    c1_done = -2
    stage_no = 0
    for c, (first, count) in enumerate(CHUNKS):
        quads = []
        for p in range(done_pieces, need[c]):
            for d in range(3):
                incoming[d, p].wait_recv()
            begin, size = pieces[p]
            quads = list(range(begin // 4, (begin + size) // 4))
        done_pieces = need[c]
        if quads:
            for q in quads:
                pack(q)
            pk = send_pack(c + 1, quads)
        if c > 0:
            for copy in layers[c - 1]:
                copy.wait_recv()
            results[c - 1] = finish_chunk(c - 1)
        if quads:
            for copy in pk:
                copy.wait_recv()
            for q in quads:
                strips(q)
        end = first + count + 2
        if c == 0:
            lat[0].wait_recv()

            @pl.when(la == 0)
            def _():
                for g in range(5):
                    for kk in range(2):
                        for r in range(HALO):
                            c0[g, kk, 8 * r : 8 * r + 8] = zero_tile

        if c == len(CHUNKS) - 1:
            lat[1].wait_recv()

            @pl.when(la == n_lat - 1)
            def _():
                for g in range(5):
                    for kk in range(2):
                        for r in range(rows + HALO, rows + 2 * HALO):
                            c0[g, kk, 8 * r : 8 * r + 8] = zero_tile

        step(c0, c1, c1_done, end - c1_done, False)
        c1_done = end
        step(c1, c2, first, count, True)
        layers[c] = send_layers(c)

        if c == 0:
            stage.wait_recv()
            h1[1, own] = h_in[...] - (DT * 0.5) * (dp[1] + dp_got[1])
            edges = [
                go(remote(h1.at[1, own], h1.at[0, own], h_s.at[0], h_r.at[0], {"lon": east})),
                go(remote(h1.at[1, own], h1.at[2, own], h_s.at[1], h_r.at[1], {"lon": west})),
                go(remote(h1.at[1, top], h1.at[1, pl.ds(0, 8)], h_s.at[2], h_r.at[2], {"lat": north})),
                go(remote(h1.at[1, low], h1.at[1, pl.ds(rows + 8, 8)], h_s.at[3], h_r.at[3], {"lat": south})),
            ]

    for copy in layers[-1]:
        copy.wait_recv()
    results[-1] = finish_chunk(len(CHUNKS) - 1)

    for copy in edges:
        copy.wait_recv()

    @pl.when(la == 0)
    def _():
        h1[1, 0:8] = jnp.zeros((8, width), F32)

    @pl.when(la == n_lat - 1)
    def _():
        h1[1, rows + 8 : rows + 16] = jnp.zeros((8, width), F32)

    for b in (0, 2):
        h1[b, 0:8] = jnp.zeros((8, width), F32)
        h1[b, rows + 8 : rows + 16] = jnp.zeros((8, width), F32)
    wide_h = jnp.concatenate([h1[0], h1[1], h1[2]], axis=1)
    div = jnp.zeros((rows, width), F32)
    for kk in range(2):
        u, v = mom[kk], mom[2 + kk]
        div = div + divergence(u, v)
        new_u, new_v = momentum(u, v, wide_h, wet_of((2 * t + kk).astype(F32), wide_depth))
        o_u[kk] = new_u[8 : 8 + rows, width : 2 * width]
        o_v[kk] = new_v[8 : 8 + rows, width : 2 * width]
    dp[2] = div
    stage = dp_stage(2)
    stage.wait_recv()
    dp[3] = dp[2] + dp_got[2]
    stage = dp_stage(3)

    def unturn(src, first, count):
        for kk in range(2):
            for n in range(8):
                o_x[n, 2 * src + kk, pl.ds(first, count)] = ry[src, kk, pl.ds(8 * first + n, count, stride=8), :]

    unpacked = 0
    for c, (first, count) in enumerate(CHUNKS):
        copies, here = results[c]
        here.wait()
        end = (first + count) // 8 * 8
        unturn(t, unpacked, end - unpacked)
        for copy, d in zip(copies, (1, 0, 2)):
            copy.wait_recv()
            unturn(source[d], unpacked, end - unpacked)
        unpacked = end
        if c == 0:
            stage.wait_recv()
            o_h[...] = h1[1, own] - (DT * 0.5) * (dp[3] + dp_got[3])
    for copy in sends:
        copy.wait_send()


def body(x, u, v, th, h, w, table, pace, uptake):
    tracers, levels, rows, width = x.shape
    vmem, smem = pl.BlockSpec(memory_space=pltpu.VMEM), pl.BlockSpec(memory_space=pltpu.SMEM)
    ext = rows + 2 * HALO
    n_c = len(CHUNKS)
    n_p = len(in_pieces(rows)[0])
    most = -(-max(count for _, count in CHUNKS) // 8) * 8
    dma = lambda *s: pltpu.SemaphoreType.DMA(s)
    buf = lambda *s: pltpu.VMEM(s, F32)
    scratch = [
        buf(3, 2, 8 * rows, width),
        buf(5, 2, 8 * ext, width),
        buf(5, 2, 8 * ext, width),
        buf(5, 2, 8 * ext, width),
        buf(4, 2, 8 * rows, width),
        buf(4, 2, 8 * rows, width),
        buf(2, 2, rows // 4, 8, width),
        buf(2, 2, rows // 4, 8, width),
        buf(2, 8, 2, rows + 16, width),
        buf(2, 8, 2, ext, 8, width),
        buf(3, 6, rows + 16, width),
        buf(4, rows + 16, 3 * width),
        buf(4, rows, width),
        buf(4, rows, width),
        buf(3, rows + 16, width),
        buf(2, rows, width),
        buf(n_c, most, width),
        buf(n_c, 3, most, width),
        buf(2, rows, width),
        buf(2, rows, width),
        buf(4, 8, width),
        dma(3, n_p), dma(3, n_p),
        dma(2, n_c + 1), dma(2, n_c + 1),
        dma(2), dma(2),
        dma(4), dma(4),
        dma(4), dma(4),
        dma(4), dma(4),
        dma(n_c, 3), dma(n_c, 3),
        dma(n_c, 3), dma(n_c, 3),
        dma(n_c),
    ]
    field = jax.ShapeDtypeStruct(u.shape, F32)
    return pl.pallas_call(
        kernel,
        out_shape=(
            jax.ShapeDtypeStruct(x.shape, F32), field, field, field, jax.ShapeDtypeStruct(h.shape, F32),
        ),
        in_specs=[vmem] * 7 + [smem] * 2,
        out_specs=(vmem,) * 5,
        scratch_shapes=scratch,
        compiler_params=pltpu.CompilerParams(
            collective_id=0, has_side_effects=True, vmem_limit_bytes=48 * 1024 * 1024
        ),
    )(x, u, v, th, h, w, table, pace, uptake)


def solution(mesh):
    return jax.shard_map(
        body,
        mesh=mesh,
        in_specs=(
            P("trc", None, "lat", "lon"),
            P("trc", "lat", "lon"),
            P("trc", "lat", "lon"),
            P("trc", "lat", "lon"),
            P("lat", "lon"),
            P("lat", "lon"),
            P(),
            P(),
            P(),
        ),
        out_specs=(
            P("trc", None, "lat", "lon"),
            P("trc", "lat", "lon"),
            P("trc", "lat", "lon"),
            P("trc", "lat", "lon"),
            P("lat", "lon"),
        ),
        check_vma=False,
    )
```

profile of v0, /device:TPU:8, one launch (start us, length us, event | category | flops | bytes accessed | tf_op | source)
XLA Modules:
  0.0 68.7 jit_solution(11846731491981276553)
XLA Ops:
  0.6 0.0 copy-start
  0.6 1.2 %copy-done = f32[8,8,32,128]{3,2,1,0:T(8,128)S(1)} copy-done((f32[8,8,32,128]{3,2,1,0:T(8,128)S(1)}, f32[8,8,32,128]{3,2,1,0:T(8,128)}, u32[]{:S(2)}) %copy-start) | copy-done | bytes 1048600
  1.9 0.0 copy-start.1
  1.9 0.8 %copy-done.1 = f32[2,32,128]{2,1,0:T(8,128)S(1)} copy-done((f32[2,32,128]{2,1,0:T(8,128)S(1)}, f32[2,32,128]{2,1,0:T(8,128)}, u32[]{:S(2)}) %copy-start.1) | copy-done | bytes 32792
  2.6 0.0 copy-start.2
  2.6 0.8 %copy-done.2 = f32[2,32,128]{2,1,0:T(8,128)S(1)} copy-done((f32[2,32,128]{2,1,0:T(8,128)S(1)}, f32[2,32,128]{2,1,0:T(8,128)}, u32[]{:S(2)}) %copy-start.2) | copy-done | bytes 32792
  3.4 0.0 copy-start.3
  3.4 0.8 %copy-done.3 = f32[2,32,128]{2,1,0:T(8,128)S(1)} copy-done((f32[2,32,128]{2,1,0:T(8,128)S(1)}, f32[2,32,128]{2,1,0:T(8,128)}, u32[]{:S(2)}) %copy-start.3) | copy-done | bytes 32792
  4.1 0.0 copy-start.4
  4.1 0.7 %copy-done.4 = f32[32,128]{1,0:T(8,128)S(1)} copy-done((f32[32,128]{1,0:T(8,128)S(1)}, f32[32,128]{1,0:T(8,128)}, u32[]{:S(2)}) %copy-start.4) | copy-done | bytes 16408
  4.9 0.0 copy-start.5
  4.9 0.7 %copy-done.5 = s32[32,128]{1,0:T(8,128)S(1)} copy-done((s32[32,128]{1,0:T(8,128)S(1)}, s32[32,128]{1,0:T(8,128)}, u32[]{:S(2)}) %copy-start.5) | copy-done | bytes 16408
  5.6 0.0 copy-start.6
  5.6 0.7 %copy-done.6 = f32[32,32]{1,0:T(8,128)S(1)} copy-done((f32[32,32]{1,0:T(8,128)S(1)}, f32[32,32]{1,0:T(8,128)}, u32[]{:S(2)}) %copy-start.6) | copy-done | bytes 4120
  6.3 0.0 copy-start.7
  6.3 0.7 copy-done.7
  6.9 0.0 copy-start.8
  6.9 0.7 copy-done.8
  7.6 57.7 %shard_map.128 = (f32[8,8,32,128]{3,2,1,0:T(8,128)S(1)}, f32[2,32,128]{2,1,0:T(8,128)S(1)}, f32[2,32,128]{2,1,0:T(8,128)S(1)}, f32[2,32,128]{2,1,0:T(8,128)S(1)}, f32[32,128]{1,0:T(8,128)S(1)}) custom-call(f32[8,8,32,128]{3,2,1,0:T(8,128)S(1)} %copy-done, f32[2,32,128]{2,1,0:T(8,128)S(1)} %copy-done.1, f32[2,32,128]{2,1,0:T(8,128)S(1)} %copy-done.2, ...), custom_call_target="tpu_custom_call" | custom-call | tf_op jit(solution)/shard_map/pallas_call | solution.py:555
  65.3 1.0 %copy.19 = f32[8,8,32,128]{3,2,1,0:T(8,128)} copy(f32[8,8,32,128]{3,2,1,0:T(8,128)S(1)} %get-tuple-element.10) | data formatting | bytes 2097152
  66.2 0.6 copy.20
  66.8 0.6 copy.21
  67.5 0.6 copy.22
  68.1 0.6 copy.23
Async XLA Ops:
  0.6 1.2 %copy-start = (f32[8,8,32,128]{3,2,1,0:T(8,128)S(1)}, f32[8,8,32,128]{3,2,1,0:T(8,128)}, u32[]{:S(2)}) copy-start(f32[8,8,32,128]{3,2,1,0:T(8,128)} %x.1) | copy-start | bytes 3145732
  1.9 0.8 %copy-start.1 = (f32[2,32,128]{2,1,0:T(8,128)S(1)}, f32[2,32,128]{2,1,0:T(8,128)}, u32[]{:S(2)}) copy-start(f32[2,32,128]{2,1,0:T(8,128)} %u_in.1) | copy-start | bytes 98308
  2.6 0.8 %copy-start.2 = (f32[2,32,128]{2,1,0:T(8,128)S(1)}, f32[2,32,128]{2,1,0:T(8,128)}, u32[]{:S(2)}) copy-start(f32[2,32,128]{2,1,0:T(8,128)} %v_in.1) | copy-start | bytes 98308
  3.4 0.8 %copy-start.3 = (f32[2,32,128]{2,1,0:T(8,128)S(1)}, f32[2,32,128]{2,1,0:T(8,128)}, u32[]{:S(2)}) copy-start(f32[2,32,128]{2,1,0:T(8,128)} %th_in.1) | copy-start | bytes 98308
  4.1 0.7 %copy-start.4 = (f32[32,128]{1,0:T(8,128)S(1)}, f32[32,128]{1,0:T(8,128)}, u32[]{:S(2)}) copy-start(f32[32,128]{1,0:T(8,128)} %h_in.1) | copy-start | bytes 49156
  4.9 0.7 %copy-start.5 = (s32[32,128]{1,0:T(8,128)S(1)}, s32[32,128]{1,0:T(8,128)}, u32[]{:S(2)}) copy-start(s32[32,128]{1,0:T(8,128)} %w_in.1) | copy-start | bytes 49156
  5.6 0.7 %copy-start.6 = (f32[32,32]{1,0:T(8,128)S(1)}, f32[32,32]{1,0:T(8,128)}, u32[]{:S(2)}) copy-start(f32[32,32]{1,0:T(8,128)} %table.1) | copy-start | bytes 12292
  6.3 0.7 copy-start.7
  6.9 0.7 copy-start.8
where the time goes:
time: 69.2 us; the launch traced here: 68.7 us
  Pallas kernels  57.7 us (83%)
  local copies, waits for them, and re-layouts  10.4 us (15%)
    pallas_call x1, Pallas kernels, body(): pl.pallas_call(kernel, out_shape=(jax.ShapeDtypeStruct(x.shape, F32), fie...  57.7 us
    unnamed x23, local copies, waits for them, and re-layouts  10.4 us

commit v1 on v0

--- a/solution.py
+++ b/solution.py
@@ -13,6 +13,7 @@
 DT = 0.1
 CHUNKS = ((0, 12), (12, 20))
 HALO = 4
+THROTTLE = True
 UNROLL = 4
 
 
@@ -43,12 +44,13 @@
 
 
 def kernel(
-    x, u_in, v_in, th_in, h_in, w_in, table, pace, uptake,
+    x_far, u_far, v_far, th_far, h_far, w_far, table_far, pace, uptake,
     o_x, o_u, o_v, o_t, o_h,
-    tx, c0, c1, c2, out, ry, pk_own, pk_got, cc, cf,
+    x, u_in, v_in, th_in, h_in, w_in, table,
+    tx, c0, c1, c2, out, ry, pk_own, pk_got, sk, cc, cf,
     vs, mom, dp, dp_got, h1, ab, s_own, s_got, fl, w01, prod,
-    in_s, in_r, lon_s, lon_r, lat_s, lat_r, vs_s, vs_r, dp_s, dp_r, h_s, h_r,
-    s_s, s_r, out_s, out_r, loc,
+    ready, in_s, in_r, lon_s, lon_r, sk_s, sk_r, lat_s, lat_r, vs_s, vs_r, dp_s, dp_r, h_s, h_r,
+    s_s, s_r, out_s, out_r, loc, near,
 ):
     rows, width = h_in.shape
     n_lat, n_lon = lax.axis_size("lat"), lax.axis_size("lon")
@@ -72,9 +74,18 @@
         return copy
 
     barrier = pltpu.get_barrier_semaphore()
-    friends = [{"trc": g} for g in other] + [{"lon": east}, {"lon": west}, {"lat": north}, {"lat": south}]
+    friends = [{"trc": g} for g in other] + [{"lon": west}, {"lat": north}, {"lat": south}]
     for friend in friends:
         pl.semaphore_signal(barrier, inc=1, device_id=friend, device_id_type=MESH)
+
+    fetched = []
+    for i, (far, close) in enumerate(
+        ((u_far, u_in), (v_far, v_in), (h_far, h_in), (w_far, w_in), (x_far, x), (th_far, th_in), (table_far, table))
+    ):
+        fetched.append(pltpu.make_async_copy(far, close, near.at[i]))
+        fetched[-1].start()
+    for copy in fetched[:4]:
+        copy.wait()
 
     depth = w_in[...].astype(F32)
 
@@ -89,37 +100,67 @@
     vs[1, 4, own] = h_in[...]
     vs[1, 5, own] = depth
 
-    def turn(target, dst, base):
+    lane = lax.broadcasted_iota(jnp.int32, (8, width), 1)
+    slot = lane // 8
+    lane32 = lane % 32
+    n_half = rows // 16
+    fetched[4].wait()
+
+    @pl.loop(0, 4)
+    def _(target):
         for kk in range(2):
             for n in range(8):
-                dst[kk, pl.ds(base + n, rows, stride=8), :] = x[n, 2 * target + kk]
-
+                tx[target, kk, pl.ds(n, rows, stride=8), :] = x[n, 2 * target + kk]
+
+    @pl.loop(0, 4)
+    def _(target):
+        for kk in range(2):
+            for half in range(n_half):
+                to_west = to_east = jnp.zeros((8, width), F32)
+                for j in range(16):
+                    turned = lanes(tx[target, kk, pl.ds(8 * (16 * half + j), 8), :], 8 * (j + 1))
+                    to_west = jnp.where(slot == (j + 1) % 16, turned, to_west)
+                    to_east = jnp.where(slot == j, turned, to_east)
+                pk_own[0, 2 * target + kk, half] = to_west
+                pk_own[1, 2 * target + kk, half] = to_east
+
+    mine = pltpu.make_async_copy(tx.at[t], c0.at[t, :, pl.ds(8 * HALO, 8 * rows)], loc.at[len(CHUNKS)])
+    mine.start()
+    fetched[5].wait()
+    fetched[6].wait()
     pl.semaphore_wait(barrier, len(friends))
+    pl.semaphore_signal(ready, inc=1, device_id={"lon": east}, device_id_type=MESH)
     vs_lon = [
         go(remote(vs.at[1, :, own], vs.at[0, :, own], vs_s.at[0], vs_r.at[0], {"lon": east})),
-        go(remote(vs.at[1, :, own], vs.at[2, :, own], vs_s.at[1], vs_r.at[1], {"lon": west})),
     ]
+    pk = [go(remote(pk_own.at[1], pk_got.at[1], lon_s.at[0], lon_r.at[0], {"lon": east}))]
     incoming = {}
 
     def send_piece(d, p):
         first, count = pieces[p]
         incoming[d, p] = go(
             remote(
-                tx.at[d, :, pl.ds(8 * first, 8 * count)],
+                tx.at[other[d], :, pl.ds(8 * first, 8 * count)],
                 c0.at[t, :, pl.ds(8 * (first + HALO), 8 * count)],
                 in_s.at[d, p], in_r.at[d, p], {"trc": other[d]},
             )
         )
 
-    for d in (1, 0, 2):
-        turn(other[d], tx.at[d], 0)
-        send_piece(d, 0)
-        send_piece(d, 1)
-    turn(t, c0.at[t], 8 * HALO)
-    for p in range(2, len(pieces)):
-        for d in (1, 0, 2):
-            send_piece(d, p)
-
+    def send_pieces(p):
+        if p < len(pieces):
+            for d in (1, 0, 2):
+                send_piece(d, p)
+
+    send_pieces(0)
+    send_pieces(1)
+    send_pieces(2)
+    if not THROTTLE:
+        for p in range(3, len(pieces)):
+            send_pieces(p)
+
+    pl.semaphore_wait(ready, 1)
+    vs_lon.append(go(remote(vs.at[1, :, own], vs.at[2, :, own], vs_s.at[1], vs_r.at[1], {"lon": west})))
+    pk.append(go(remote(pk_own.at[0], pk_got.at[0], lon_s.at[1], lon_r.at[1], {"lon": west})))
     for copy in vs_lon:
         copy.wait_recv()
     top, low = pl.ds(rows, 8), pl.ds(8, 8)
@@ -128,52 +169,41 @@
         go(remote(vs.at[:, :, low], vs.at[:, :, pl.ds(rows + 8, 8)], vs_s.at[3], vs_r.at[3], {"lat": south})),
     ]
 
-    lane = lax.broadcasted_iota(jnp.int32, (8, width), 1)
-    slot = lane // 8
-    lane32 = lane % 32
+    for copy in pk:
+        copy.wait_recv()
+    strip_in = [
+        go(remote(pk_got.at[:, pl.ds(2 * other[d], 2)], sk.at[:, t], sk_s.at[d], sk_r.at[d], {"trc": other[d]}))
+        for d in range(3)
+    ]
+    mine_too = pltpu.make_async_copy(pk_got.at[:, pl.ds(2 * t, 2)], sk.at[:, t], loc.at[len(CHUNKS) + 1])
+    mine_too.start()
 
     def tile(buf, g, kk, r):
         return buf[g, kk, pl.ds(pl.multiple_of(8 * (r + HALO), 8), 8), :]
 
-    def pack(q):
-        pos = (q + 1) % (rows // 4)
-        for kk in range(2):
-            to_west = to_east = jnp.zeros((8, width), F32)
-            for j in range(4):
+    def strips(begin, end):
+        @pl.loop(begin, end)
+        def _(r):
+            half, j = r // 16, r % 16
+            for kk in range(2):
+                strip = jnp.zeros((8, width), F32)
                 for g in range(4):
-                    s = 4 * g + j
-                    turned = lanes(tile(c0, g, kk, 4 * q + j), 8 * (s + 1))
-                    to_west = jnp.where(slot == (s + 1) % 16, turned, to_west)
-                    to_east = jnp.where(slot == s, turned, to_east)
-            pk_own[0, kk, pos] = to_west
-            pk_own[1, kk, pos] = to_east
-
-    def send_pack(i, quads):
-        pos = [(q + 1) % (rows // 4) for q in quads]
-        part = pl.ds(min(pos), len(pos))
-        return [
-            go(remote(pk_own.at[1, :, part], pk_got.at[1, :, part], lon_s.at[0, i], lon_r.at[0, i], {"lon": east})),
-            go(remote(pk_own.at[0, :, part], pk_got.at[0, :, part], lon_s.at[1, i], lon_r.at[1, i], {"lon": west})),
-        ]
-
-    def strips(q):
-        pos = (q + 1) % (rows // 4)
-        for kk in range(2):
-            from_west, from_east = pk_got[1, kk, pos], pk_got[0, kk, pos]
-            own_w, own_e = pk_own[0, kk, pos], pk_own[1, kk, pos]
-            for j in range(4):
-                left = lanes(jnp.where(slot % 4 == j, from_west, own_w), -8 * j)
-                right = lanes(jnp.where(slot % 4 == j, own_e, from_east), 16 - 8 * j)
-                c0[4, kk, pl.ds(8 * (4 * q + j + HALO), 8), :] = jnp.where(lane32 < 16, left, right)
+                    here = tile(c0, g, kk, r)
+                    parts = (
+                        pltpu.roll(sk[1, g, kk, half], (32 * g + width - 8 * j) % width, 1),
+                        lanes(here, 32 * g + 8),
+                        lanes(here, 32 * g + 24),
+                        pltpu.roll(sk[0, g, kk, half], (32 * g + 16 + width - 8 * j) % width, 1),
+                    )
+                    for i, part in enumerate(parts):
+                        strip = jnp.where(slot == 4 * g + i, part, strip)
+                c0[4, kk, pl.ds(pl.multiple_of(8 * (r + HALO), 8), 8), :] = strip
 
     for p in (0, 1):
         for d in range(3):
             incoming[d, p].wait_recv()
-    last = rows // 4 - 1
-    pack(last)
-    pack(0)
-    pk = send_pack(0, (last, 0))
-
+    if THROTTLE:
+        send_pieces(3)
     for copy in vs_lat:
         copy.wait_recv()
 
@@ -260,10 +290,12 @@
     dp[0] = div
     stage = dp_stage(0)
 
-    for copy in pk:
+    mine.wait()
+    mine_too.wait()
+    for copy in strip_in:
         copy.wait_recv()
-    strips(last)
-    strips(0)
+    strips(0, HALO)
+    strips(rows - HALO, rows)
     lat = [
         go(remote(c0.at[:, :, pl.ds(8 * rows, 8 * HALO)], c0.at[:, :, pl.ds(0, 8 * HALO)],
                   lat_s.at[0], lat_r.at[0], {"lat": north})),
@@ -287,7 +319,8 @@
         prod[g] = column(pace, g)
 
     def step(src, dst, first, count, finish):
-        for kk in range(2):
+        @pl.loop(0, 2)
+        def _(kk):
             def coef(form, i, r):
                 return cf[form, i, kk, r + HALO]
 
@@ -394,32 +427,24 @@
         return copies, here
 
     zero_tile = jnp.zeros((8, width), F32)
-    done_pieces, done_quads = 2, 1
+    done_pieces = 2
     layers = [None] * len(CHUNKS)
     results = [None] * len(CHUNKS)
     c1_done = -2
     stage_no = 0
     for c, (first, count) in enumerate(CHUNKS):
-        quads = []
         for p in range(done_pieces, need[c]):
             for d in range(3):
                 incoming[d, p].wait_recv()
             begin, size = pieces[p]
-            quads = list(range(begin // 4, (begin + size) // 4))
+            if THROTTLE:
+                send_pieces(p + 2)
+            strips(begin, begin + size)
         done_pieces = need[c]
-        if quads:
-            for q in quads:
-                pack(q)
-            pk = send_pack(c + 1, quads)
         if c > 0:
             for copy in layers[c - 1]:
                 copy.wait_recv()
             results[c - 1] = finish_chunk(c - 1)
-        if quads:
-            for copy in pk:
-                copy.wait_recv()
-            for q in quads:
-                strips(q)
         end = first + count + 2
         if c == 0:
             lat[0].wait_recv()
@@ -455,10 +480,6 @@
                 go(remote(h1.at[1, top], h1.at[1, pl.ds(0, 8)], h_s.at[2], h_r.at[2], {"lat": north})),
                 go(remote(h1.at[1, low], h1.at[1, pl.ds(rows + 8, 8)], h_s.at[3], h_r.at[3], {"lat": south})),
             ]
-
-    for copy in layers[-1]:
-        copy.wait_recv()
-    results[-1] = finish_chunk(len(CHUNKS) - 1)
 
     for copy in edges:
         copy.wait_recv()
@@ -484,6 +505,10 @@
         o_v[kk] = new_v[8 : 8 + rows, width : 2 * width]
     dp[2] = div
     stage = dp_stage(2)
+    for copy in layers[-1]:
+        copy.wait_recv()
+    results[-1] = finish_chunk(len(CHUNKS) - 1)
+
     stage.wait_recv()
     dp[3] = dp[2] + dp_got[2]
     stage = dp_stage(3)
@@ -510,6 +535,28 @@
         copy.wait_send()
 
 
+def place(*refs):
+    far, to, near, come, leave = refs[:5], refs[5:10], refs[10:15], refs[15], refs[16]
+    moves = []
+    for i in range(5):
+        parts = [slice(None)] if i else [pl.ds(2 * p, 2) for p in range(4)]
+        for part in parts:
+            n = len(moves)
+            moves.append(
+                (
+                    pltpu.make_async_copy(far[i].at[part], near[i].at[part], come.at[n]),
+                    pltpu.make_async_copy(near[i].at[part], to[i].at[part], leave.at[n]),
+                )
+            )
+    for first, _ in moves:
+        first.start()
+    for first, second in moves:
+        first.wait()
+        second.start()
+    for _, second in moves:
+        second.wait()
+
+
 def body(x, u, v, th, h, w, table, pace, uptake):
     tracers, levels, rows, width = x.shape
     vmem, smem = pl.BlockSpec(memory_space=pltpu.VMEM), pl.BlockSpec(memory_space=pltpu.SMEM)
@@ -520,14 +567,16 @@
     dma = lambda *s: pltpu.SemaphoreType.DMA(s)
     buf = lambda *s: pltpu.VMEM(s, F32)
     scratch = [
-        buf(3, 2, 8 * rows, width),
+        *(pltpu.VMEM(a.shape, a.dtype) for a in (x, u, v, th, h, w, table)),
+        buf(4, 2, 8 * rows, width),
         buf(5, 2, 8 * ext, width),
         buf(5, 2, 8 * ext, width),
         buf(5, 2, 8 * ext, width),
         buf(4, 2, 8 * rows, width),
         buf(4, 2, 8 * rows, width),
-        buf(2, 2, rows // 4, 8, width),
-        buf(2, 2, rows // 4, 8, width),
+        buf(2, 8, rows // 16, 8, width),
+        buf(2, 8, rows // 16, 8, width),
+        buf(2, 4, 2, rows // 16, 8, width),
         buf(2, 8, 2, rows + 16, width),
         buf(2, 8, 2, ext, 8, width),
         buf(3, 6, rows + 16, width),
@@ -541,29 +590,40 @@
         buf(2, rows, width),
         buf(2, rows, width),
         buf(4, 8, width),
+        pltpu.SemaphoreType.REGULAR,
         dma(3, n_p), dma(3, n_p),
-        dma(2, n_c + 1), dma(2, n_c + 1),
+        dma(2), dma(2),
+        dma(3), dma(3),
         dma(2), dma(2),
         dma(4), dma(4),
         dma(4), dma(4),
         dma(4), dma(4),
         dma(n_c, 3), dma(n_c, 3),
         dma(n_c, 3), dma(n_c, 3),
-        dma(n_c),
+        dma(n_c + 2), dma(7),
     ]
     field = jax.ShapeDtypeStruct(u.shape, F32)
-    return pl.pallas_call(
+    results = pl.pallas_call(
         kernel,
         out_shape=(
             jax.ShapeDtypeStruct(x.shape, F32), field, field, field, jax.ShapeDtypeStruct(h.shape, F32),
         ),
-        in_specs=[vmem] * 7 + [smem] * 2,
+        in_specs=[pl.BlockSpec(memory_space=pltpu.HBM)] * 7 + [smem] * 2,
         out_specs=(vmem,) * 5,
         scratch_shapes=scratch,
         compiler_params=pltpu.CompilerParams(
-            collective_id=0, has_side_effects=True, vmem_limit_bytes=48 * 1024 * 1024
+            collective_id=0, has_side_effects=True, vmem_limit_bytes=62 * 1024 * 1024
         ),
     )(x, u, v, th, h, w, table, pace, uptake)
+
+    return pl.pallas_call(
+        place,
+        out_shape=tuple(jax.ShapeDtypeStruct(r.shape, F32) for r in results),
+        in_specs=[pl.BlockSpec(memory_space=pltpu.HBM)] * 5,
+        out_specs=(pl.BlockSpec(memory_space=pltpu.HBM),) * 5,
+        scratch_shapes=[*(pltpu.VMEM(r.shape, F32) for r in results), dma(8), dma(8)],
+        compiler_params=pltpu.CompilerParams(vmem_limit_bytes=62 * 1024 * 1024),
+    )(*results)
 
 
 def solution(mesh):

time: 69.2 us -> 58.3 us (0.84)
  local copies, waits for them, and re-layouts: 10.4 us -> 0 us
    unnamed x23 -> x0, local copies, waits for them, and re-layouts: 10.4 us -> none
    pallas_call x1, Pallas kernels: 57.7 us -> 55.5 us  [body(): pl.pallas_call(kernel, out_shape=(jax.ShapeDtypeStruct(x.shape, F32), fie...]
    pallas_call x0 -> x1, Pallas kernels: none -> 2.07 us  [body(): pl.pallas_call(place, out_shape=tuple((jax.ShapeDtypeStruct(r.shape, F32)...]
where the time goes in v1:
time: 58.3 us; the launch traced here: 58.2 us
  Pallas kernels  57.5 us (99%)
  between operations  0.64 us (1%)
    pallas_call x1, Pallas kernels, body(): pl.pallas_call(kernel, out_shape=(jax.ShapeDtypeStruct(x.shape, F32), fie...  55.5 us
    pallas_call x1, Pallas kernels, body(): pl.pallas_call(place, out_shape=tuple((jax.ShapeDtypeStruct(r.shape, F32)...  2.07 us

profile of v1, /device:TPU:8, one launch (start us, length us, event | category | flops | bytes accessed | tf_op | source)
XLA Modules:
  0.0 58.2 jit_solution(5283820448571424846)
XLA Ops:
  0.6 55.5 %shard_map.128 = (f32[8,8,32,128]{3,2,1,0:T(8,128)}, f32[2,32,128]{2,1,0:T(8,128)}, f32[2,32,128]{2,1,0:T(8,128)}, f32[2,32,128]{2,1,0:T(8,128)}, f32[32,128]{1,0:T(8,128)}) custom-call(f32[8,8,32,128]{3,2,1,0:T(8,128)} %x_far.1, f32[2,32,128]{2,1,0:T(8,128)} %u_far.1, f32[2,32,128]{2,1,0:T(8,128)} %v_far.1, f32[2,32,128]{2,1,0:T(8,128)} %th_far.1, ...), custom_call_target="tpu_custom_call" | custom-call | tf_op jit(solution)/shard_map/pallas_call | solution.py:606
  56.1 2.1 %shard_map.129 = (f32[8,8,32,128]{3,2,1,0:T(8,128)}, f32[2,32,128]{2,1,0:T(8,128)}, f32[2,32,128]{2,1,0:T(8,128)}, f32[2,32,128]{2,1,0:T(8,128)}, f32[32,128]{1,0:T(8,128)}) custom-call(f32[8,8,32,128]{3,2,1,0:T(8,128)} %get-tuple-element.10.refs_0_, f32[2,32,128]{2,1,0:T(8,128)} %get-tuple-element.11.refs_1_, f32[2,32,128]{2,1,0:T(8,128)} %get-tuple-element.12.refs_2_, ...), custom_call_target="tpu_custom_call" | custom-call | tf_op jit(solution)/shard_map/pallas_call | solution.py:619

commit v2 on v1

--- a/solution.py
+++ b/solution.py
@@ -11,10 +11,13 @@
 MESH = pl.DeviceIdType.MESH
 F32 = jnp.float32
 DT = 0.1
-CHUNKS = ((0, 12), (12, 20))
+CHUNKS = ((0, 16), (16, 16))
+PARTS = (((0, 8), (8, 8)), ((16, 8), (24, 8)))
+N_PARTS = sum(len(p) for p in PARTS)
 HALO = 4
 THROTTLE = True
-UNROLL = 4
+ROUNDS = 2
+GROUPS = ((0, 1, 2, 3, 4),)
 
 
 def in_pieces(rows):
@@ -45,12 +48,13 @@
 
 def kernel(
     x_far, u_far, v_far, th_far, h_far, w_far, table_far, pace, uptake,
+    far_x, far_u, far_v, far_t, far_h,
     o_x, o_u, o_v, o_t, o_h,
     x, u_in, v_in, th_in, h_in, w_in, table,
     tx, c0, c1, c2, out, ry, pk_own, pk_got, sk, cc, cf,
-    vs, mom, dp, dp_got, h1, ab, s_own, s_got, fl, w01, prod,
+    vs, ve_own, ve_got, mom, dp, dp_got, h1, ab, s_own, s_got, fl, w01, prod,
     ready, in_s, in_r, lon_s, lon_r, sk_s, sk_r, lat_s, lat_r, vs_s, vs_r, dp_s, dp_r, h_s, h_r,
-    s_s, s_r, out_s, out_r, loc, near,
+    s_s, s_r, out_s, out_r, loc, near, away,
 ):
     rows, width = h_in.shape
     n_lat, n_lon = lax.axis_size("lat"), lax.axis_size("lon")
@@ -103,35 +107,43 @@
     lane = lax.broadcasted_iota(jnp.int32, (8, width), 1)
     slot = lane // 8
     lane32 = lane % 32
-    n_half = rows // 16
+    slot4 = lane // 4
     fetched[4].wait()
 
     @pl.loop(0, 4)
     def _(target):
         for kk in range(2):
+            fields = [x[n, 2 * target + kk] for n in range(8)]
             for n in range(8):
-                tx[target, kk, pl.ds(n, rows, stride=8), :] = x[n, 2 * target + kk]
+                tx[target, kk, pl.ds(n, rows, stride=8), :] = fields[n]
 
     @pl.loop(0, 4)
     def _(target):
         for kk in range(2):
-            for half in range(n_half):
-                to_west = to_east = jnp.zeros((8, width), F32)
-                for j in range(16):
-                    turned = lanes(tx[target, kk, pl.ds(8 * (16 * half + j), 8), :], 8 * (j + 1))
-                    to_west = jnp.where(slot == (j + 1) % 16, turned, to_west)
-                    to_east = jnp.where(slot == j, turned, to_east)
-                pk_own[0, 2 * target + kk, half] = to_west
-                pk_own[1, 2 * target + kk, half] = to_east
-
-    mine = pltpu.make_async_copy(tx.at[t], c0.at[t, :, pl.ds(8 * HALO, 8 * rows)], loc.at[len(CHUNKS)])
+            to_west = to_east = jnp.zeros((8, width), F32)
+            for j in range(rows):
+                turned = lanes(tx[target, kk, pl.ds(8 * j, 8), :], 4 * (j + 1))
+                to_west = jnp.where(slot4 == (j + 1) % 32, turned, to_west)
+                to_east = jnp.where(slot4 == j, turned, to_east)
+            pk_own[0, 2 * target + kk] = to_west
+            pk_own[1, 2 * target + kk] = to_east
+
+    lane_v = lax.broadcasted_iota(jnp.int32, (rows, width), 1) // 8
+    to_west = to_east = jnp.zeros((rows, width), F32)
+    for f in range(6):
+        field = vs[1, f, own]
+        to_west = jnp.where(lane_v == f, lanes(field, 8 * f), to_west)
+        to_east = jnp.where(lane_v == f, lanes(field, 8 * f + 8), to_east)
+    ve_own[0], ve_own[1] = to_west, to_east
+
+    mine = pltpu.make_async_copy(tx.at[t], c0.at[t, :, pl.ds(8 * HALO, 8 * rows)], loc.at[N_PARTS])
     mine.start()
     fetched[5].wait()
     fetched[6].wait()
     pl.semaphore_wait(barrier, len(friends))
     pl.semaphore_signal(ready, inc=1, device_id={"lon": east}, device_id_type=MESH)
     vs_lon = [
-        go(remote(vs.at[1, :, own], vs.at[0, :, own], vs_s.at[0], vs_r.at[0], {"lon": east})),
+        go(remote(ve_own.at[1], ve_got.at[1], vs_s.at[0], vs_r.at[0], {"lon": east})),
     ]
     pk = [go(remote(pk_own.at[1], pk_got.at[1], lon_s.at[0], lon_r.at[0], {"lon": east}))]
     incoming = {}
@@ -159,10 +171,13 @@
             send_pieces(p)
 
     pl.semaphore_wait(ready, 1)
-    vs_lon.append(go(remote(vs.at[1, :, own], vs.at[2, :, own], vs_s.at[1], vs_r.at[1], {"lon": west})))
+    vs_lon.append(go(remote(ve_own.at[0], ve_got.at[0], vs_s.at[1], vs_r.at[1], {"lon": west})))
     pk.append(go(remote(pk_own.at[0], pk_got.at[0], lon_s.at[1], lon_r.at[1], {"lon": west})))
     for copy in vs_lon:
         copy.wait_recv()
+    for f in range(6):
+        vs[0, f, own] = lanes(ve_got[1], width - 8 - 8 * f)
+        vs[2, f, own] = lanes(ve_got[0], -8 * f)
     top, low = pl.ds(rows, 8), pl.ds(8, 8)
     vs_lat = [
         go(remote(vs.at[:, :, top], vs.at[:, :, pl.ds(0, 8)], vs_s.at[2], vs_r.at[2], {"lat": north})),
@@ -175,35 +190,53 @@
         go(remote(pk_got.at[:, pl.ds(2 * other[d], 2)], sk.at[:, t], sk_s.at[d], sk_r.at[d], {"trc": other[d]}))
         for d in range(3)
     ]
-    mine_too = pltpu.make_async_copy(pk_got.at[:, pl.ds(2 * t, 2)], sk.at[:, t], loc.at[len(CHUNKS) + 1])
+    mine_too = pltpu.make_async_copy(pk_got.at[:, pl.ds(2 * t, 2)], sk.at[:, t], loc.at[N_PARTS + 1])
     mine_too.start()
 
     def tile(buf, g, kk, r):
         return buf[g, kk, pl.ds(pl.multiple_of(8 * (r + HALO), 8), 8), :]
 
     def strips(begin, end):
-        @pl.loop(begin, end)
-        def _(r):
-            half, j = r // 16, r % 16
-            for kk in range(2):
-                strip = jnp.zeros((8, width), F32)
-                for g in range(4):
-                    here = tile(c0, g, kk, r)
-                    parts = (
-                        pltpu.roll(sk[1, g, kk, half], (32 * g + width - 8 * j) % width, 1),
-                        lanes(here, 32 * g + 8),
-                        lanes(here, 32 * g + 24),
-                        pltpu.roll(sk[0, g, kk, half], (32 * g + 16 + width - 8 * j) % width, 1),
-                    )
-                    for i, part in enumerate(parts):
-                        strip = jnp.where(slot == 4 * g + i, part, strip)
-                c0[4, kk, pl.ds(pl.multiple_of(8 * (r + HALO), 8), 8), :] = strip
+        @pl.loop(0, (end - begin) // 4)
+        def _(quad):
+            results = []
+            for i in range(4):
+                r = begin + 4 * quad + i
+                for kk in range(2):
+                    strip = jnp.zeros((8, width), F32)
+                    for g in range(4):
+                        here = tile(c0, g, kk, r)
+                        parts = (
+                            pltpu.roll(sk[1, g, kk], (32 * g + 4 + width - 4 * r) % width, 1),
+                            lanes(here, 32 * g + 8),
+                            lanes(here, 32 * g + 24),
+                            pltpu.roll(sk[0, g, kk], (32 * g + 20 + width - 4 * r) % width, 1),
+                        )
+                        for n, part in enumerate(parts):
+                            strip = jnp.where(slot == 4 * g + n, part, strip)
+                    results.append(strip)
+            for i in range(4):
+                for kk in range(2):
+                    put = pl.ds(pl.multiple_of(8 * (begin + 4 * quad + i + HALO), 8), 8)
+                    c0[4, kk, put, :] = results[2 * i + kk]
 
     for p in (0, 1):
         for d in range(3):
             incoming[d, p].wait_recv()
     if THROTTLE:
         send_pieces(3)
+    mine.wait()
+    mine_too.wait()
+    for copy in strip_in:
+        copy.wait_recv()
+    strips(0, HALO)
+    strips(rows - HALO, rows)
+    lat = [
+        go(remote(c0.at[:, :, pl.ds(8 * rows, 8 * HALO)], c0.at[:, :, pl.ds(0, 8 * HALO)],
+                  lat_s.at[0], lat_r.at[0], {"lat": north})),
+        go(remote(c0.at[:, :, pl.ds(8 * HALO, 8 * HALO)], c0.at[:, :, pl.ds(8 * (rows + HALO), 8 * HALO)],
+                  lat_s.at[1], lat_r.at[1], {"lat": south})),
+    ]
     for copy in vs_lat:
         copy.wait_recv()
 
@@ -251,10 +284,10 @@
 
     @pl.loop(1, rows + 2 * HALO)
     def _(r):
-        for form in range(2):
-            for i in range(8):
-                for kk in range(2):
-                    cf[form, i, kk, r] = jnp.broadcast_to(cc[form, i, kk, pl.ds(r + 8 - HALO, 1), :], (8, width))
+        every = [(form, i, kk) for form in range(2) for i in range(8) for kk in range(2)]
+        wide_rows = [jnp.broadcast_to(cc[f, i, kk, pl.ds(r + 8 - HALO, 1), :], (8, width)) for f, i, kk in every]
+        for (f, i, kk), value in zip(every, wide_rows):
+            cf[f, i, kk, r] = value
 
     big = rows + 16
     row_no = (la * rows - 8 + lax.broadcasted_iota(jnp.int32, (big, 1), 0)).astype(F32)
@@ -290,18 +323,6 @@
     dp[0] = div
     stage = dp_stage(0)
 
-    mine.wait()
-    mine_too.wait()
-    for copy in strip_in:
-        copy.wait_recv()
-    strips(0, HALO)
-    strips(rows - HALO, rows)
-    lat = [
-        go(remote(c0.at[:, :, pl.ds(8 * rows, 8 * HALO)], c0.at[:, :, pl.ds(0, 8 * HALO)],
-                  lat_s.at[0], lat_r.at[0], {"lat": north})),
-        go(remote(c0.at[:, :, pl.ds(8 * HALO, 8 * HALO)], c0.at[:, :, pl.ds(8 * (rows + HALO), 8 * HALO)],
-                  lat_s.at[1], lat_r.at[1], {"lat": south})),
-    ]
     stage.wait_recv()
     dp[1] = dp[0] + dp_got[0]
     stage = dp_stage(1)
@@ -318,57 +339,77 @@
     for g in range(4):
         prod[g] = column(pace, g)
 
-    def step(src, dst, first, count, finish):
+    def step(src, dst, first, count):
         @pl.loop(0, 2)
         def _(kk):
-            def coef(form, i, r):
-                return cf[form, i, kk, r + HALO]
-
-            def face_y(form, r, a, s_a, b, s_b):
-                return (coef(form, 4, r) * a + coef(form, 5, r) * s_a) + (coef(form, 6, r) * b + coef(form, 7, r) * s_b)
-
-            start = []
-            for g in range(5):
-                q = [tile(src, g, kk, first + i) for i in (-2, -1, 0, 1)]
-                d = [q[i + 1] - q[i] for i in range(3)]
-                s = [minmod(d[0], d[1]), minmod(d[1], d[2])]
-                start.append((q[2], q[3], d[2], s[1], face_y(g // 4, first - 1, q[1], s[0], q[2], s[1])))
-
-            def one(r, state):
-                result, after = [], []
-                for g in range(5):
-                    form = g // 4
-                    c, c_n, d_n, s, g_s = state[g]
-                    c_nn = tile(src, g, kk, r + 2)
-                    d_nn = c_nn - c_n
-                    s_n = minmod(d_nn, d_n)
-                    g_n = face_y(form, r, c, s, c_n, s_n)
-                    d_e = lanes(c, -1) - c
-                    s_x = minmod(d_e, lanes(d_e, 1))
-                    right = coef(form, 0, r) * c + coef(form, 1, r) * s_x
-                    left = coef(form, 2, r) * c + coef(form, 3, r) * s_x
-                    new = c - ((right + lanes(left, -1)) - (lanes(right, 1) + left)) - (g_n - g_s)
-                    result.append(new)
-                    after.append((c_n, c_nn, d_nn, s_n, g_n))
-                if finish:
+            for groups in GROUPS:
+                def coef(form, i, r):
+                    return cf[form, i, kk, r + HALO]
+
+                def face_y(form, r, a, s_a, b, s_b):
+                    return (coef(form, 4, r) * a + coef(form, 5, r) * s_a) + (
+                        coef(form, 6, r) * b + coef(form, 7, r) * s_b
+                    )
+
+                start = []
+                for g in groups:
+                    q = [tile(src, g, kk, first + i) for i in (-2, -1, 0, 1)]
+                    d = [q[i + 1] - q[i] for i in range(3)]
+                    s = [minmod(d[0], d[1]), minmod(d[1], d[2])]
+                    start.append((q[2], q[3], d[2], s[1], face_y(g // 4, first - 1, q[1], s[0], q[2], s[1])))
+
+                unroll = count // ROUNDS
+
+                def some(i, state):
+                    base = first + unroll * i
+                    ahead = [[tile(src, g, kk, base + j + 2) for g in groups] for j in range(unroll)]
+                    results = []
+                    for j in range(unroll):
+                        r = base + j
+                        after = []
+                        for g, c_nn, (c, c_n, d_n, s, g_s) in zip(groups, ahead[j], state):
+                            form = g // 4
+                            d_nn = c_nn - c_n
+                            s_n = minmod(d_nn, d_n)
+                            g_n = face_y(form, r, c, s, c_n, s_n)
+                            d_e = lanes(c, -1) - c
+                            s_x = minmod(d_e, lanes(d_e, 1))
+                            right = coef(form, 0, r) * c + coef(form, 1, r) * s_x
+                            left = coef(form, 2, r) * c + coef(form, 3, r) * s_x
+                            results.append(
+                                c - ((right + lanes(left, -1)) - (lanes(right, 1) + left)) - (g_n - g_s)
+                            )
+                            after.append((c_n, c_nn, d_nn, s_n, g_n))
+                        state = tuple(after)
+                    for j in range(unroll):
+                        for n, g in enumerate(groups):
+                            put = pl.ds(pl.multiple_of(8 * (base + j + HALO), 8), 8)
+                            dst[g, kk, put, :] = results[j * len(groups) + n]
+                    return state
+
+                lax.fori_loop(0, ROUNDS, some, tuple(start))
+
+    def absorb(first, count):
+        @pl.loop(0, count // 4)
+        def _(i):
+            for kk in range(2):
+                results = []
+                for j in range(4):
+                    r = first + 4 * i + j
+                    strip = tile(c2, 4, kk, r)
                     total = jnp.zeros((8, width), F32)
                     for g in range(4):
-                        new = jnp.where(lane < 4, lanes(result[4], -(32 * g + 8)), result[g])
-                        new = jnp.where(lane >= width - 4, lanes(result[4], width - 24 - 32 * g), new)
-                        dst[g, kk, pl.ds(pl.multiple_of(8 * (r + HALO), 8), 8), :] = new
+                        new = tile(c2, g, kk, r)
+                        new = jnp.where(lane < 4, lanes(strip, -(32 * g + 8)), new)
+                        new = jnp.where(lane >= width - 4, lanes(strip, width - 24 - 32 * g), new)
+                        results.append(new)
                         total = total + uptakes[g] * jnp.abs(new)
-                    ab[kk, pl.ds(r, 1), :] = jnp.sum(total, axis=0, keepdims=True)
-                else:
-                    for g in range(5):
-                        dst[g, kk, pl.ds(pl.multiple_of(8 * (r + HALO), 8), 8), :] = result[g]
-                return tuple(after)
-
-            def some(i, state):
-                for j in range(UNROLL):
-                    state = one(first + UNROLL * i + j, state)
-                return state
-
-            lax.fori_loop(0, count // UNROLL, some, tuple(start))
+                    results.append(jnp.sum(total, axis=0, keepdims=True))
+                for j in range(4):
+                    r = first + 4 * i + j
+                    for g in range(4):
+                        c2[g, kk, pl.ds(pl.multiple_of(8 * (r + HALO), 8), 8), :] = results[5 * j + g]
+                    ab[kk, pl.ds(r, 1), :] = results[5 * j + 4]
 
     def layer(kk, first, count):
         dep = vs[1, 5, pl.ds(8 + first, count)]
@@ -398,33 +439,40 @@
             w01[kk, part] = DT * wet
             above = above + lay
         matrix = table[...]
-
-        @pl.loop(0, count // 4)
-        def _(i):
-            for kk in range(2):
-                r0 = first + 4 * i
-                stacked = jnp.concatenate(
-                    [jnp.concatenate([tile(c2, g, kk, r0 + j) for g in range(4)], axis=0) for j in range(4)], axis=1
-                )
-                mixed = jnp.dot(matrix, stacked, precision=lax.Precision.HIGHEST, preferred_element_type=F32)
-                for j in range(4):
-                    light = fl[kk, pl.ds(r0 + j, 1), :]
-                    wet = w01[kk, pl.ds(r0 + j, 1), :]
-                    for g in range(4):
-                        moved = tile(c2, g, kk, r0 + j)
-                        mix = mixed[8 * g : 8 * g + 8, width * j : width * (j + 1)]
-                        out[g, kk, pl.ds(pl.multiple_of(8 * (r0 + j), 8), 8), :] = (
-                            moved + wet * mix + light * (prod[g] * moved)
-                        )
-
-        part8 = pl.ds(8 * first, 8 * count)
-        copies = [
-            go(remote(out.at[other[d], :, part8], ry.at[t, :, part8], out_s.at[c, d], out_r.at[c, d], {"trc": other[d]}))
-            for d in (1, 0, 2)
-        ]
-        here = pltpu.make_async_copy(out.at[t, :, part8], ry.at[t, :, part8], loc.at[c])
-        here.start()
-        return copies, here
+        copies = []
+        for n, (begin, size) in enumerate(PARTS[c]):
+
+            @pl.loop(0, size // 4)
+            def _(i):
+                for kk in range(2):
+                    r0 = begin + 4 * i
+                    stacked = jnp.concatenate(
+                        [jnp.concatenate([tile(c2, g, kk, r0 + j) for g in range(4)], axis=0) for j in range(4)],
+                        axis=1,
+                    )
+                    mixed = jnp.dot(matrix, stacked, precision=lax.Precision.HIGHEST, preferred_element_type=F32)
+                    results = []
+                    for j in range(4):
+                        light = fl[kk, pl.ds(r0 + j, 1), :]
+                        wet = w01[kk, pl.ds(r0 + j, 1), :]
+                        for g in range(4):
+                            moved = stacked[8 * g : 8 * g + 8, width * j : width * (j + 1)]
+                            mix = mixed[8 * g : 8 * g + 8, width * j : width * (j + 1)]
+                            results.append(moved + wet * mix + light * (prod[g] * moved))
+                    for j in range(4):
+                        for g in range(4):
+                            out[g, kk, pl.ds(pl.multiple_of(8 * (r0 + j), 8), 8), :] = results[4 * j + g]
+
+            part8 = pl.ds(8 * begin, 8 * size)
+            s = sum(len(p) for p in PARTS[:c]) + n
+            copies.append([
+                go(remote(out.at[other[d], :, part8], ry.at[t, :, part8], out_s.at[s, d], out_r.at[s, d], {"trc": other[d]}))
+                for d in (1, 0, 2)
+            ])
+            here = pltpu.make_async_copy(out.at[t, :, part8], ry.at[t, :, part8], loc.at[s])
+            here.start()
+            copies[-1].append(here)
+        return copies
 
     zero_tile = jnp.zeros((8, width), F32)
     done_pieces = 2
@@ -441,10 +489,6 @@
                 send_pieces(p + 2)
             strips(begin, begin + size)
         done_pieces = need[c]
-        if c > 0:
-            for copy in layers[c - 1]:
-                copy.wait_recv()
-            results[c - 1] = finish_chunk(c - 1)
         end = first + count + 2
         if c == 0:
             lat[0].wait_recv()
@@ -466,9 +510,14 @@
                         for r in range(rows + HALO, rows + 2 * HALO):
                             c0[g, kk, 8 * r : 8 * r + 8] = zero_tile
 
-        step(c0, c1, c1_done, end - c1_done, False)
+        step(c0, c1, c1_done, end - c1_done)
         c1_done = end
-        step(c1, c2, first, count, True)
+        if c > 0:
+            for copy in layers[c - 1]:
+                copy.wait_recv()
+            results[c - 1] = finish_chunk(c - 1)
+        step(c1, c2, first, count)
+        absorb(first, count)
         layers[c] = send_layers(c)
 
         if c == 0:
@@ -515,22 +564,41 @@
 
     def unturn(src, first, count):
         for kk in range(2):
+            fields = [ry[src, kk, pl.ds(8 * first + n, count, stride=8), :] for n in range(8)]
             for n in range(8):
-                o_x[n, 2 * src + kk, pl.ds(first, count)] = ry[src, kk, pl.ds(8 * first + n, count, stride=8), :]
-
-    unpacked = 0
-    for c, (first, count) in enumerate(CHUNKS):
-        copies, here = results[c]
-        here.wait()
-        end = (first + count) // 8 * 8
-        unturn(t, unpacked, end - unpacked)
-        for copy, d in zip(copies, (1, 0, 2)):
-            copy.wait_recv()
-            unturn(source[d], unpacked, end - unpacked)
-        unpacked = end
-        if c == 0:
-            stage.wait_recv()
-            o_h[...] = h1[1, own] - (DT * 0.5) * (dp[3] + dp_got[3])
+                o_x[n, 2 * src + kk, pl.ds(first, count)] = fields[n]
+
+    leaving = []
+
+    def leave(near_ref, far_ref):
+        leaving.append(pltpu.make_async_copy(near_ref, far_ref, away.at[len(leaving)]))
+        leaving[-1].start()
+
+    leave(o_u, far_u)
+    leave(o_v, far_v)
+    leave(o_t, far_t)
+    unpacked, part_no = 0, 0
+    for c in range(len(CHUNKS)):
+        for n, (first, count) in enumerate(PARTS[c]):
+            *copies, here = results[c][n]
+            end = (first + count) // 8 * 8
+            part = pl.ds(unpacked, end - unpacked)
+            for copy, src in ((here, t), *((copies[i], source[d]) for i, d in enumerate((1, 0, 2)))):
+                if copy is here:
+                    copy.wait()
+                else:
+                    copy.wait_recv()
+                if end > unpacked:
+                    unturn(src, unpacked, end - unpacked)
+                    leave(o_x.at[:, pl.ds(2 * src, 2), part], far_x.at[:, pl.ds(2 * src, 2), part])
+            unpacked = end
+            part_no += 1
+            if part_no == N_PARTS - 1:
+                stage.wait_recv()
+                o_h[...] = h1[1, own] - (DT * 0.5) * (dp[3] + dp_got[3])
+                leave(o_h, far_h)
+    for copy in leaving:
+        copy.wait()
     for copy in sends:
         copy.wait_send()
 
@@ -559,7 +627,7 @@
 
 def body(x, u, v, th, h, w, table, pace, uptake):
     tracers, levels, rows, width = x.shape
-    vmem, smem = pl.BlockSpec(memory_space=pltpu.VMEM), pl.BlockSpec(memory_space=pltpu.SMEM)
+    smem = pl.BlockSpec(memory_space=pltpu.SMEM)
     ext = rows + 2 * HALO
     n_c = len(CHUNKS)
     n_p = len(in_pieces(rows)[0])
@@ -567,6 +635,7 @@
     dma = lambda *s: pltpu.SemaphoreType.DMA(s)
     buf = lambda *s: pltpu.VMEM(s, F32)
     scratch = [
+        *(pltpu.VMEM(a.shape, F32) for a in (x, u, u, u, h)),
         *(pltpu.VMEM(a.shape, a.dtype) for a in (x, u, v, th, h, w, table)),
         buf(4, 2, 8 * rows, width),
         buf(5, 2, 8 * ext, width),
@@ -574,12 +643,14 @@
         buf(5, 2, 8 * ext, width),
         buf(4, 2, 8 * rows, width),
         buf(4, 2, 8 * rows, width),
-        buf(2, 8, rows // 16, 8, width),
-        buf(2, 8, rows // 16, 8, width),
-        buf(2, 4, 2, rows // 16, 8, width),
+        buf(2, 8, 8, width),
+        buf(2, 8, 8, width),
+        buf(2, 4, 2, 8, width),
         buf(2, 8, 2, rows + 16, width),
         buf(2, 8, 2, ext, 8, width),
         buf(3, 6, rows + 16, width),
+        buf(2, rows, width),
+        buf(2, rows, width),
         buf(4, rows + 16, 3 * width),
         buf(4, rows, width),
         buf(4, rows, width),
@@ -599,8 +670,8 @@
         dma(4), dma(4),
         dma(4), dma(4),
         dma(n_c, 3), dma(n_c, 3),
-        dma(n_c, 3), dma(n_c, 3),
-        dma(n_c + 2), dma(7),
+        dma(N_PARTS, 3), dma(N_PARTS, 3),
+        dma(N_PARTS + 2), dma(7), dma(4 + 4 * N_PARTS),
     ]
     field = jax.ShapeDtypeStruct(u.shape, F32)
     results = pl.pallas_call(
@@ -609,7 +680,7 @@
             jax.ShapeDtypeStruct(x.shape, F32), field, field, field, jax.ShapeDtypeStruct(h.shape, F32),
         ),
         in_specs=[pl.BlockSpec(memory_space=pltpu.HBM)] * 7 + [smem] * 2,
-        out_specs=(vmem,) * 5,
+        out_specs=(pl.BlockSpec(memory_space=pltpu.HBM),) * 5,
         scratch_shapes=scratch,
         compiler_params=pltpu.CompilerParams(
             collective_id=0, has_side_effects=True, vmem_limit_bytes=62 * 1024 * 1024

time: 58.3 us -> 49.8 us (0.85); the launches traced: 58.2 us -> 48.9 us
  Pallas kernels: 57.5 us -> 48.2 us
    pallas_call x1, Pallas kernels: 55.5 us -> 46.2 us  [body(): pl.pallas_call(kernel, out_shape=(jax.ShapeDtypeStruct(x.shape, F32), fie...]
where the time goes in v2:
time: 49.8 us; the launch traced here: 48.9 us
  Pallas kernels  48.2 us (97%)
  between operations  0.64 us (1%)
    pallas_call x1, Pallas kernels, body(): pl.pallas_call(kernel, out_shape=(jax.ShapeDtypeStruct(x.shape, F32), fie...  46.2 us
    pallas_call x1, Pallas kernels, body(): pl.pallas_call(place, out_shape=tuple((jax.ShapeDtypeStruct(r.shape, F32)...  2.07 us

profile of v2, /device:TPU:8, one launch (start us, length us, event | category | flops | bytes accessed | tf_op | source)
XLA Modules:
  0.0 48.9 jit_solution(14305669087457518428)
XLA Ops:
  0.6 46.2 %shard_map.128 = (f32[8,8,32,128]{3,2,1,0:T(8,128)}, f32[2,32,128]{2,1,0:T(8,128)}, f32[2,32,128]{2,1,0:T(8,128)}, f32[2,32,128]{2,1,0:T(8,128)}, f32[32,128]{1,0:T(8,128)}) custom-call(f32[8,8,32,128]{3,2,1,0:T(8,128)} %x_far.1, f32[2,32,128]{2,1,0:T(8,128)} %u_far.1, f32[2,32,128]{2,1,0:T(8,128)} %v_far.1, f32[2,32,128]{2,1,0:T(8,128)} %th_far.1, ...), custom_call_target="tpu_custom_call" | custom-call | tf_op jit(solution)/shard_map/pallas_call | solution.py:677
  46.8 2.1 %shard_map.129 = (f32[8,8,32,128]{3,2,1,0:T(8,128)}, f32[2,32,128]{2,1,0:T(8,128)}, f32[2,32,128]{2,1,0:T(8,128)}, f32[2,32,128]{2,1,0:T(8,128)}, f32[32,128]{1,0:T(8,128)}) custom-call(f32[8,8,32,128]{3,2,1,0:T(8,128)} %get-tuple-element.10.refs_0_, f32[2,32,128]{2,1,0:T(8,128)} %get-tuple-element.11.refs_1_, f32[2,32,128]{2,1,0:T(8,128)} %get-tuple-element.12.refs_2_, ...), custom_call_target="tpu_custom_call" | custom-call | tf_op jit(solution)/shard_map/pallas_call | solution.py:690

commit v3 on v2

--- a/solution.py
+++ b/solution.py
@@ -11,8 +11,8 @@
 MESH = pl.DeviceIdType.MESH
 F32 = jnp.float32
 DT = 0.1
-CHUNKS = ((0, 16), (16, 16))
-PARTS = (((0, 8), (8, 8)), ((16, 8), (24, 8)))
+CHUNKS = ((0, 12), (12, 20))
+PARTS = (((0, 12),), ((12, 8), (20, 12)))
 N_PARTS = sum(len(p) for p in PARTS)
 HALO = 4
 THROTTLE = True
@@ -282,11 +282,14 @@
             for i, w in enumerate(weights(ay)):
                 cc[form, 4 + i, kk] = w
 
-    @pl.loop(1, rows + 2 * HALO)
-    def _(r):
-        every = [(form, i, kk) for form in range(2) for i in range(8) for kk in range(2)]
-        wide_rows = [jnp.broadcast_to(cc[f, i, kk, pl.ds(r + 8 - HALO, 1), :], (8, width)) for f, i, kk in every]
-        for (f, i, kk), value in zip(every, wide_rows):
+    @pl.loop(0, (rows + 2 * HALO - 1) // 3)
+    def _(three):
+        every = [
+            (form, i, kk, 1 + 3 * three + n)
+            for n in range(3) for form in range(2) for i in range(8) for kk in range(2)
+        ]
+        wide_rows = [jnp.broadcast_to(cc[f, i, kk, pl.ds(r + 8 - HALO, 1), :], (8, width)) for f, i, kk, r in every]
+        for (f, i, kk, r), value in zip(every, wide_rows):
             cf[f, i, kk, r] = value
 
     big = rows + 16

time: 49.8 us -> 49 us (0.984); the launches traced: 48.9 us -> 48.8 us
  no operation moved by 1% of the time
where the time goes in v3:
time: 49 us; the launch traced here: 48.8 us
  Pallas kernels  48.1 us (98%)
  between operations  0.64 us (1%)
    pallas_call x1, Pallas kernels, body(): pl.pallas_call(kernel, out_shape=(jax.ShapeDtypeStruct(x.shape, F32), fie...  46 us
    pallas_call x1, Pallas kernels, body(): pl.pallas_call(place, out_shape=tuple((jax.ShapeDtypeStruct(r.shape, F32)...  2.07 us

profile of v3, /device:TPU:8, one launch (start us, length us, event | category | flops | bytes accessed | tf_op | source)
XLA Modules:
  0.0 48.8 jit_solution(5954879824146126774)
XLA Ops:
  0.6 46.0 %shard_map.128 = (f32[8,8,32,128]{3,2,1,0:T(8,128)}, f32[2,32,128]{2,1,0:T(8,128)}, f32[2,32,128]{2,1,0:T(8,128)}, f32[2,32,128]{2,1,0:T(8,128)}, f32[32,128]{1,0:T(8,128)}) custom-call(f32[8,8,32,128]{3,2,1,0:T(8,128)} %x_far.1, f32[2,32,128]{2,1,0:T(8,128)} %u_far.1, f32[2,32,128]{2,1,0:T(8,128)} %v_far.1, f32[2,32,128]{2,1,0:T(8,128)} %th_far.1, ...), custom_call_target="tpu_custom_call" | custom-call | tf_op jit(solution)/shard_map/pallas_call | solution.py:680
  46.7 2.1 %shard_map.129 = (f32[8,8,32,128]{3,2,1,0:T(8,128)}, f32[2,32,128]{2,1,0:T(8,128)}, f32[2,32,128]{2,1,0:T(8,128)}, f32[2,32,128]{2,1,0:T(8,128)}, f32[32,128]{1,0:T(8,128)}) custom-call(f32[8,8,32,128]{3,2,1,0:T(8,128)} %get-tuple-element.10.refs_0_, f32[2,32,128]{2,1,0:T(8,128)} %get-tuple-element.11.refs_1_, f32[2,32,128]{2,1,0:T(8,128)} %get-tuple-element.12.refs_2_, ...), custom_call_target="tpu_custom_call" | custom-call | tf_op jit(solution)/shard_map/pallas_call | solution.py:693
